TPU v7x, 32 devices: a whole 2x2x4 slice. The times are simulated.
32 devices in a mesh: groups: 2 (over y), pairs: 4 (over z), sub: 2 (over x), rep: 2 (over core).
Axes of the slice: x: 2, y: 2, z: 4, core: 2. Of those that a mesh axis runs over, the one named last changes fastest.
Arguments:
- integrals: bfloat16 [384, 128, 1024], P(('groups', 'pairs'), 'sub'), parts along dimension 0, may hold values from -0.21875 to 0.21875
- density: bfloat16 [384, 32, 1024], P(('groups', 'pairs'), 'rep'), parts along dimension 0, may hold values from -6 to 6
- block_owner: int32 [384], P(('groups', 'pairs')), parts along dimension 0, may hold values from 0 to 3, as said below
Outputs:
- coulomb: float32 [384, 32, 1024], P(('groups', 'pairs'), 'rep', 'sub'), parts along dimension 0
There are 2 independent parts, one for each index of `groups`. A program takes and returns all parts, laid end to end along the dimension named above; each array names one. Nothing has to cross between parts.
Inputs may be any that keep to these rules, and one draw needn't show every extreme that they name: Block k sits in the integral slots of pair owner block_owner[k]; in the rows of one device no owner is named more than 24 times and some owner exactly 24 times; over all rows every owner is named exactly 48 times.
All inputs are finite; a program needn't handle non-finite values.
Results may differ from a plain program's by a relative error of at most 0.0029.
Values may be sent and summed in bfloat16 or wider, within the bound.
A program may use at most 64 MiB of HBM per device.

v0:
```python
import jax
import jax.numpy as jnp
from jax import lax
from jax.sharding import PartitionSpec as P


def on_device(integrals, density, block_owner):
    npairs = lax.axis_size("pairs")
    blocks = density.shape[0]
    dens_dev = density.shape[1]
    block_width = density.shape[2]
    capacity = 2 * blocks // npairs
    peer_ids = jnp.arange(npairs, dtype=jnp.int32)
    onehot = (block_owner[:, None] == peer_ids[None, :]).astype(jnp.int32)
    before = jnp.cumsum(onehot, axis=0) - onehot
    rank_in = jnp.sum(before * onehot, axis=1)
    outgoing = block_owner * capacity + rank_in
    buffer_ids = jnp.arange(npairs * capacity, dtype=jnp.int32)
    matches = (outgoing[None, :] == buffer_ids[:, None]).astype(jnp.int32)
    filled = jnp.sum(matches, axis=1)
    source_ids = jnp.sum(matches * jnp.arange(blocks, dtype=jnp.int32)[None, :], axis=1)
    packed = jnp.where(filled[:, None, None] > 0, density[source_ids], jnp.zeros((), density.dtype))
    packed = packed.reshape(npairs, capacity, dens_dev, block_width)
    arrived, arrived_flags = (
        lax.all_to_all(packed, "pairs", split_axis=0, concat_axis=0, tiled=True),
        lax.all_to_all(
            filled.reshape(npairs, capacity), "pairs", split_axis=0, concat_axis=0, tiled=True
        ),
    )
    counts = jnp.sum(arrived_flags, axis=1)
    finish = jnp.cumsum(counts)
    starts = finish - counts
    slot_ids = jnp.arange(blocks, dtype=jnp.int32)
    anchor = jnp.sum((finish[None, :] <= slot_ids[:, None]).astype(jnp.int32), axis=1)
    anchor_onehot = (anchor[:, None] == peer_ids[None, :]).astype(jnp.int32)
    offsets = slot_ids - jnp.sum(anchor_onehot * starts[None, :], axis=1)
    places = anchor * capacity + offsets
    slot_density = arrived.reshape(npairs * capacity, dens_dev, block_width)[places]
    partial_fit = jnp.einsum(
        "jpx,jdx->pd", integrals, slot_density, preferred_element_type=jnp.float32
    )
    fitted = lax.psum(partial_fit, "pairs").astype(jnp.bfloat16)
    slot_coulomb = jnp.einsum("pd,jpx->jdx", fitted, integrals, preferred_element_type=jnp.float32)
    return_index = jnp.clip(
        starts[:, None] + jnp.arange(capacity, dtype=jnp.int32)[None, :], 0, blocks - 1
    ).reshape(-1)
    return_flags = arrived_flags.reshape(-1)
    gathered = slot_coulomb[return_index]
    kept = jnp.where(return_flags[:, None, None] > 0, gathered, jnp.zeros((), jnp.float32))
    homeward = lax.all_to_all(
        kept.reshape(npairs, capacity, dens_dev, slot_coulomb.shape[2]),
        "pairs",
        split_axis=0,
        concat_axis=0,
        tiled=True,
    )
    own_blocks = homeward.reshape(npairs * capacity, dens_dev, block_width)[outgoing]
    coulomb = lax.psum_scatter(own_blocks, "sub", scatter_dimension=2, tiled=True)
    return coulomb


def solution(mesh):
    in_specs = (
        P(("groups", "pairs"), "sub", None),
        P(("groups", "pairs"), "rep", None),
        P(("groups", "pairs")),
    )
    out_specs = P(("groups", "pairs"), "rep", "sub")
    return jax.shard_map(
        on_device, mesh=mesh, in_specs=in_specs, out_specs=out_specs, check_vma=False
    )
```

profile of v0, /device:TPU:9, one launch (start us, length us, event | category | flops | bytes accessed | tf_op | source)
XLA Modules:
  0.0 325.0 jit_solution(14077020261420094116)
XLA Ops:
  6.5 0.8 fusion
  7.5 0.8 select_reduce_fusion.2
  8.3 0.7 compare_select_fusion
  9.0 0.1 convert_reduce_fusion
  9.1 0.7 all_to_all.12
  9.7 4.8 %all-to-all-start = ((s32[4,1,24]{2,1,0:T(1,128)}), s32[4,1,24]{2,1,0:T(1,128)S(1)}, u32[]{:S(2)}, u32[]{:S(2)}) async-start(s32[4,1,24]{2,1,0:T(1,128)} %bitcast), calls=%async_computation | async-start | bytes 4096 | tf_op jit(solution)/shard_map/all_to_all | solution.py:26
  14.5 0.1 gt.25
  14.6 2.6 gather_fusion
  17.2 3.8 %broadcast_select_fusion.1 = bf16[4,24,16,1024]{3,2,1,0:T(8,128)(2,1)} fusion(bf16[4,24,16,1024]{3,2,1,0:T(8,128)(2,1)} %bitcast.40, pred[4,24]{1,0:T(4,128)(4,1)S(1)} %gt.25), kind=kLoop, calls=%fused_computation.5 | loop fusion | flops 1572864 | bytes 6291552 | tf_op jit(solution)/shard_map/jit(_where)/select_n | solution.py:22
  21.0 4.6 %all-to-all-start.1 = ((bf16[4,24,16,1024]{3,2,1,0:T(8,128)(2,1)}), bf16[4,24,16,1024]{3,2,1,0:T(8,128)(2,1)}, u32[]{:S(2)}, u32[]{:S(2)}) async-start(bf16[4,24,16,1024]{3,2,1,0:T(8,128)(2,1)} %broadcast_select_fusion.1), calls=%async_computation.1 | async-start | bytes 6291456 | tf_op jit(solution)/shard_map/all_to_all | solution.py:25
  25.7 0.2 reduce_sum.62
  25.8 0.2 reduce-window.7
  26.3 0.2 select_reduce_fusion
  26.5 65.4 %all-to-all-done.1 = bf16[4,24,16,1024]{3,2,1,0:T(8,128)(2,1)} async-done(((bf16[4,24,16,1024]{3,2,1,0:T(8,128)(2,1)}), bf16[4,24,16,1024]{3,2,1,0:T(8,128)(2,1)}, u32[]{:S(2)}, u32[]{:S(2)}) %all-to-all-start.1) | async-done | bytes 3145760 | tf_op jit(solution)/shard_map/all_to_all | solution.py:25
  91.9 2.5 gather_fusion.1
  94.5 4.5 %convolution_bitcast_fusion.1 = f32[64,16]{0,1:T(8,128)S(1)} fusion(bf16[48,16,1024]{2,1,0:T(8,128)(2,1)S(1)} %gather_fusion.1, bf16[48,64,1024]{2,1,0:T(8,128)(2,1)} %param.3), kind=kOutput, calls=%fused_computation.7 | convolution fusion | flops 100663296 | bytes 7868416 | tf_op jit(solution)/shard_map/jpx,jdx->pd/dot_general | solution.py:39
  99.0 10.7 %psum.7 = bf16[64,16]{0,1:T(8,128)(2,1)S(1)} all-reduce(f32[64,16]{0,1:T(8,128)S(1)} %convolution_bitcast_fusion.1), channel_id=1, replica_groups=mesh['groups'=2,'pairs'=4,'sub'=2,'rep'=2] {'pairs'}, use_global_device_ids=true, to_apply=%region_8.9 | all-reduce | flops 1024 | bytes 6144 | tf_op jit(solution)/shard_map/psum | solution.py:42
  109.6 5.4 %convolution_bitcast_fusion = f32[48,16,1024]{2,1,0:T(8,128)} fusion(bf16[48,64,1024]{2,1,0:T(8,128)(2,1)} %param.3, bf16[64,16]{0,1:T(8,128)(2,1)S(1)} %psum.7), kind=kOutput, calls=%fused_computation.6 | convolution fusion | flops 100663296 | bytes 9439232 | tf_op jit(solution)/shard_map/pd,jpx->jdx/dot_general | solution.py:43
  115.1 5.5 %gather_fusion.2 = f32[96,16,1024]{2,1,0:T(8,128)} fusion(f32[48,16,1024]{2,1,0:T(8,128)} %convolution_bitcast_fusion, s32[1024]{0:T(1024)S(1)} %pad_clamp_fusion.1), kind=kCustom, calls=%fused_computation.2 | custom fusion | bytes 12583296 | tf_op jit(solution)/shard_map/gather | solution.py:48
  120.6 5.9 %broadcast_select_fusion = f32[4,24,16,1024]{3,2,1,0:T(8,128)} fusion(f32[4,24,16,1024]{3,2,1,0:T(8,128)} %bitcast.39, pred[4,24]{1,0:T(4,128)(4,1)S(1)} %bitcast.41), kind=kLoop, calls=%fused_computation.4 | loop fusion | flops 1572864 | bytes 12583008 | tf_op jit(solution)/shard_map/jit(_where)/select_n | solution.py:49
  126.5 5.6 %all-to-all-start.2 = ((f32[4,24,16,1024]{3,2,1,0:T(8,128)}), f32[4,24,16,1024]{3,2,1,0:T(8,128)}, u32[]{:S(2)}, u32[]{:S(2)}) async-start(f32[4,24,16,1024]{3,2,1,0:T(8,128)} %broadcast_select_fusion), calls=%async_computation.2 | async-start | bytes 12582912 | tf_op jit(solution)/shard_map/all_to_all | solution.py:50
  132.1 130.7 %all-to-all-done.2 = f32[4,24,16,1024]{3,2,1,0:T(8,128)} async-done(((f32[4,24,16,1024]{3,2,1,0:T(8,128)}), f32[4,24,16,1024]{3,2,1,0:T(8,128)}, u32[]{:S(2)}, u32[]{:S(2)}) %all-to-all-start.2) | async-done | bytes 6291488 | tf_op jit(solution)/shard_map/all_to_all | solution.py:50
  262.8 5.2 %gather_fusion.3 = f32[48,16,1024]{2,1,0:T(8,128)} fusion(f32[96,16,1024]{2,1,0:T(8,128)} %bitcast.16, s32[1024]{0:T(1024)S(1)} %pad_clamp_fusion), kind=kCustom, calls=%fused_computation.3 | custom fusion | bytes 6291648 | tf_op jit(solution)/shard_map/gather | solution.py:57
  268.1 50.1 %reduce-scatter.2.cloned.1.call-done = f32[48,16,512]{2,1,0:T(8,128)} async-done(((f32[48,16,1024]{2,1,0:T(8,128)}), f32[48,16,512]{2,1,0:T(8,128)}) %reduce-scatter.2.cloned.1.call-update) | async-done | bytes 1572880 | tf_op jit(solution)/shard_map/reduce_scatter | solution.py:58
  (20 shorter events, 0.4 us)
Async XLA Ops:
  6.5 8.1 %copy-start = (bf16[48,16,1024]{2,1,0:T(8,128)(2,1)S(1)}, bf16[48,16,1024]{2,1,0:T(8,128)(2,1)}, u32[]{:S(2)}) copy-start(bf16[48,16,1024]{2,1,0:T(8,128)(2,1)} %param.4) | copy-start | bytes 4718596
  9.7 11.3 %all-to-all-start = ((s32[4,1,24]{2,1,0:T(1,128)}), s32[4,1,24]{2,1,0:T(1,128)S(1)}, u32[]{:S(2)}, u32[]{:S(2)}) async-start(s32[4,1,24]{2,1,0:T(1,128)} %bitcast), calls=%async_computation | async-start | bytes 4096 | tf_op jit(solution)/shard_map/all_to_all | solution.py:26
  21.0 70.9 %all-to-all-start.1 = ((bf16[4,24,16,1024]{3,2,1,0:T(8,128)(2,1)}), bf16[4,24,16,1024]{3,2,1,0:T(8,128)(2,1)}, u32[]{:S(2)}, u32[]{:S(2)}) async-start(bf16[4,24,16,1024]{3,2,1,0:T(8,128)(2,1)} %broadcast_select_fusion.1), calls=%async_computation.1 | async-start | bytes 6291456 | tf_op jit(solution)/shard_map/all_to_all | solution.py:25
  126.5 136.3 %all-to-all-start.2 = ((f32[4,24,16,1024]{3,2,1,0:T(8,128)}), f32[4,24,16,1024]{3,2,1,0:T(8,128)}, u32[]{:S(2)}, u32[]{:S(2)}) async-start(f32[4,24,16,1024]{3,2,1,0:T(8,128)} %broadcast_select_fusion), calls=%async_computation.2 | async-start | bytes 12582912 | tf_op jit(solution)/shard_map/all_to_all | solution.py:50
  132.1 186.1 %reduce-scatter.2.cloned.1.call-start = ((), (), s32[]{:S(2)}) async-start(), calls=%async_computation.4 | async-start | bytes 4718592 | tf_op jit(solution)/shard_map/reduce_scatter | solution.py:58
Sparse Core Ops, SparseCore 0:
  268.2 49.9 reduce-scatter.1
where the time goes:
time: 327 us; the launch traced here: 325 us
  waiting for transfers between devices  246 us (75%)
  local copies, waits for them, and re-layouts  16.7 us (5%)
  starting transfers between devices  15 us (5%)
  between operations  13.5 us (4%)
  other arithmetic  13 us (4%)
  blocking collectives  10.7 us (3%)
  matrix products  9.93 us (3%)
    all_to_all x1, waiting for transfers between devices, on_device(): lax.all_to_all(kept.reshape(npairs, capacity, dens_dev, slot_coulomb.shap...  131 us
    all_to_all x1, waiting for transfers between devices, on_device(): lax.all_to_all(packed, 'pairs', split_axis=0, concat_axis=0, tiled=True)  65.4 us
    reduce_scatter x1, waiting for transfers between devices, on_device(): lax.psum_scatter(own_blocks, 'sub', scatter_dimension=2, tiled=True)  50.1 us
    psum x1, blocking collectives, on_device(): fitted = lax.psum(partial_fit, 'pairs').astype(jnp.bfloat16)  10.7 us
  transfers between devices with their start and end apart: 4, of which 3 were waited for; matrix products, arithmetic and copies ran while one was open for 2% of the time, Pallas kernels for 0%

commit v1 on v0

v1 whole, which is shorter than its diff:
```python
import jax
import jax.numpy as jnp
from jax import lax
from jax.sharding import PartitionSpec as P


def on_device(integrals, density, block_owner):
    npairs = lax.axis_size("pairs")
    nsub = lax.axis_size("sub")
    blocks = density.shape[0]
    dens_dev = density.shape[1]
    width = density.shape[2] // nsub
    capacity = 2 * blocks // npairs
    integrals = lax.all_to_all(integrals, "sub", split_axis=2, concat_axis=1, tiled=True)
    density = lax.dynamic_slice_in_dim(density, lax.axis_index("sub") * width, width, axis=2)
    peer_ids = jnp.arange(npairs, dtype=jnp.int32)
    onehot = (block_owner[:, None] == peer_ids[None, :]).astype(jnp.int32)
    before = jnp.cumsum(onehot, axis=0) - onehot
    rank_in = jnp.sum(before * onehot, axis=1)
    outgoing = block_owner * capacity + rank_in
    buffer_ids = jnp.arange(npairs * capacity, dtype=jnp.int32)
    matches = (outgoing[None, :] == buffer_ids[:, None]).astype(jnp.int32)
    source_ids = jnp.sum(matches * jnp.arange(blocks, dtype=jnp.int32)[None, :], axis=1)
    packed = density[source_ids].reshape(npairs, capacity, dens_dev, width)
    arrived = lax.all_to_all(packed, "pairs", split_axis=0, concat_axis=0, tiled=True)
    sent = jnp.sum(onehot, axis=0)
    counts = lax.all_to_all(sent, "pairs", split_axis=0, concat_axis=0, tiled=True)
    finish = jnp.cumsum(counts)
    starts = finish - counts
    slot_ids = jnp.arange(blocks, dtype=jnp.int32)
    anchor = jnp.sum((finish[None, :] <= slot_ids[:, None]).astype(jnp.int32), axis=1)
    anchor_onehot = (anchor[:, None] == peer_ids[None, :]).astype(jnp.int32)
    offsets = slot_ids - jnp.sum(anchor_onehot * starts[None, :], axis=1)
    places = anchor * capacity + offsets
    slot_density = arrived.reshape(npairs * capacity, dens_dev, width)[places]
    partial_fit = jnp.einsum(
        "jpx,jdx->pd", integrals, slot_density, preferred_element_type=jnp.float32
    )
    fitted = lax.psum(partial_fit, ("pairs", "sub")).astype(jnp.bfloat16)
    slot_coulomb = jnp.einsum(
        "pd,jpx->jdx", fitted, integrals, preferred_element_type=jnp.float32
    ).astype(jnp.bfloat16)
    return_index = jnp.clip(
        starts[:, None] + jnp.arange(capacity, dtype=jnp.int32)[None, :], 0, blocks - 1
    ).reshape(-1)
    kept = slot_coulomb[return_index].reshape(npairs, capacity, dens_dev, width)
    homeward = lax.all_to_all(kept, "pairs", split_axis=0, concat_axis=0, tiled=True)
    coulomb = homeward.reshape(npairs * capacity, dens_dev, width)[outgoing]
    return coulomb.astype(jnp.float32)


def solution(mesh):
    in_specs = (
        P(("groups", "pairs"), "sub", None),
        P(("groups", "pairs"), "rep", None),
        P(("groups", "pairs")),
    )
    out_specs = P(("groups", "pairs"), "rep", "sub")
    return jax.shard_map(
        on_device, mesh=mesh, in_specs=in_specs, out_specs=out_specs, check_vma=False
    )
```

time: 327 us -> 231 us (0.71)
  the two profiles are of different devices: /device:TPU:9 before, /device:TPU:0 now
where the time goes in v1:
time: 231 us; the launch traced here: 229 us
  waiting for transfers between devices  102 us (44%)
  local copies, waits for them, and re-layouts  74.7 us (32%)
  starting transfers between devices  19.7 us (9%)
  blocking collectives  18.6 us (8%)
  matrix products  8.2 us (4%)
  other arithmetic  5.75 us (2%)
    all_to_all x1, waiting for transfers between devices, on_device(): lax.all_to_all(integrals, 'sub', split_axis=2, concat_axis=1, tiled=True)  67 us
    unnamed x7, local copies, waits for them, and re-layouts  52.8 us
    all_to_all x1, waiting for transfers between devices, on_device(): lax.all_to_all(kept, 'pairs', split_axis=0, concat_axis=0, tiled=True)  31.2 us
    psum x1, blocking collectives, on_device(): fitted = lax.psum(partial_fit, ('pairs', 'sub')).astype(jnp.bfloat16)  18.6 us
    all_to_all x1, local copies, waits for them, and re-layouts, on_device(): lax.all_to_all(integrals, 'sub', split_axis=2, concat_axis=1, tiled=True)  14.2 us
    all_to_all x1, starting transfers between devices, on_device(): lax.all_to_all(sent, 'pairs', split_axis=0, concat_axis=0, tiled=True)  6.32 us
    all_to_all x1, starting transfers between devices, on_device(): lax.all_to_all(integrals, 'sub', split_axis=2, concat_axis=1, tiled=True)  6.3 us
  transfers between devices with their start and end apart: 4, of which 4 were waited for; matrix products, arithmetic and copies ran while one was open for 17% of the time, Pallas kernels for 0%

profile of v1, /device:TPU:0, one launch (start us, length us, event | category | flops | bytes accessed | tf_op | source)
XLA Modules:
  0.0 229.4 jit_solution(17802944647013055346)
XLA Ops:
  0.0 0.8 fusion.1
  0.9 0.8 fusion.2
  1.8 0.7 copy.12
  2.5 6.3 %all-to-all-start.1 = ((s32[4,1,1]{2,1,0:T(1,128)}), s32[4,1,1]{2,1,0:T(1,128)S(1)}, u32[]{:S(2)}, u32[]{:S(2)}) async-start(s32[4,1,1]{2,1,0:T(1,128)} %copy.12), calls=%async_computation.1 | async-start | bytes 4096 | tf_op jit(solution)/shard_map/all_to_all | solution.py:27
  8.8 0.7 compare_select_fusion
  9.7 1.9 gather_fusion
  11.6 2.6 %all-to-all-done.1 = s32[4,1,1]{2,1,0:T(1,128)S(1)} async-done(((s32[4,1,1]{2,1,0:T(1,128)}), s32[4,1,1]{2,1,0:T(1,128)S(1)}, u32[]{:S(2)}, u32[]{:S(2)}) %all-to-all-start.1) | async-done | bytes 48 | tf_op jit(solution)/shard_map/all_to_all | solution.py:27
  14.2 3.6 %all-to-all-start = ((bf16[4,24,16,512]{3,2,1,0:T(8,128)(2,1)}), bf16[4,24,16,512]{3,2,1,0:T(8,128)(2,1)S(1)}, u32[]{:S(2)}, u32[]{:S(2)}) async-start(bf16[4,24,16,512]{3,2,1,0:T(8,128)(2,1)} %bitcast.46), calls=%async_computation | async-start | bytes 3145728 | tf_op jit(solution)/shard_map/all_to_all | solution.py:25
  17.7 15.7 %copy.13 = bf16[48,64,1024]{1,0,2:T(8,128)(2,1)} copy(bf16[48,64,1024]{2,1,0:T(8,128)(2,1)} %param.3) | data formatting | bytes 12582912 | tf_op args[0]
  33.5 18.7 %reshape.176 = bf16[2,2,786432]{2,1,0:T(2,128)(2,1)} reshape(bf16[1024,48,64]{2,1,0:T(8,128)(2,1)} %bitcast.45) | data formatting | bytes 12582912
  52.2 1.5 all-to-all-done
  53.7 6.3 %all-to-all-start.2 = ((bf16[2,2,786432]{2,1,0:T(2,128)(2,1)}), bf16[2,2,786432]{2,1,0:T(2,128)(2,1)}, u32[]{:S(2)}, u32[]{:S(2)}) async-start(bf16[2,2,786432]{2,1,0:T(2,128)(2,1)} %reshape.176), calls=%async_computation.2 | async-start | bytes 12582912 | tf_op jit(solution)/shard_map/all_to_all | solution.py:14
  60.8 1.5 gather_fusion.1
  62.3 67.0 %all-to-all-done.2 = bf16[2,2,786432]{2,1,0:T(2,128)(2,1)} async-done(((bf16[2,2,786432]{2,1,0:T(2,128)(2,1)}), bf16[2,2,786432]{2,1,0:T(2,128)(2,1)}, u32[]{:S(2)}, u32[]{:S(2)}) %all-to-all-start.2) | async-done | bytes 6291488 | tf_op jit(solution)/shard_map/all_to_all | solution.py:14
  129.3 18.4 %reshape.177 = bf16[1024,48,64]{2,1,0:T(8,128)(2,1)} reshape(bf16[2,2,786432]{2,1,0:T(2,128)(2,1)} %all-to-all-done.2) | data formatting | bytes 12582912
  147.7 14.2 %copy.14 = bf16[48,64,2,512]{3,1,2,0:T(8,128)(2,1)} copy(bf16[48,64,2,512]{1,0,3,2:T(8,128)(2,1)} %bitcast.44) | data formatting | bytes 12582912 | tf_op jit(solution)/shard_map/all_to_all | solution.py:14
  161.9 4.5 %convolution_bitcast_fusion = f32[128,16]{0,1:T(8,128)S(1)} fusion(bf16[48,16,512]{2,1,0:T(8,128)(2,1)S(1)} %copy-done.1, bf16[48,128,512]{2,1,0:T(8,128)(2,1)} %bitcast.42), kind=kOutput, calls=%fused_computation.6 | convolution fusion | flops 100663296 | bytes 7086080 | tf_op jit(solution)/shard_map/jpx,jdx->pd/dot_general | solution.py:36
  166.4 18.6 %psum.7 = bf16[128,16]{0,1:T(8,128)(2,1)S(1)} all-reduce(f32[128,16]{0,1:T(8,128)S(1)} %convolution_bitcast_fusion), channel_id=1, replica_groups=mesh['groups'=2,'pairs'=4,'sub'=2,'rep'=2] {'pairs','sub'}, use_global_device_ids=true, to_apply=%region_7.8 | all-reduce | flops 2048 | bytes 12288 | tf_op jit(solution)/shard_map/psum | solution.py:39
  185.0 3.7 %fusion = bf16[48,16,512]{2,1,0:T(8,128)(2,1)S(1)} fusion(bf16[48,128,512]{2,1,0:T(8,128)(2,1)} %bitcast.43, bf16[128,16]{0,1:T(8,128)(2,1)S(1)} %psum.7), kind=kOutput, calls=%fused_computation.5 | convolution fusion | flops 101056512 | bytes 7081984 | tf_op jit(solution)/shard_map/pd,jpx->jdx/dot_general | solution.py:40
  188.7 1.9 gather_fusion.2
  190.6 3.6 %all-to-all-start.3 = ((bf16[4,24,16,512]{3,2,1,0:T(8,128)(2,1)}), bf16[4,24,16,512]{3,2,1,0:T(8,128)(2,1)S(1)}, u32[]{:S(2)}, u32[]{:S(2)}) async-start(bf16[4,24,16,512]{3,2,1,0:T(8,128)(2,1)} %bitcast.47), calls=%async_computation.3 | async-start | bytes 3145728 | tf_op jit(solution)/shard_map/all_to_all | solution.py:47
  194.2 31.2 %all-to-all-done.3 = bf16[4,24,16,512]{3,2,1,0:T(8,128)(2,1)S(1)} async-done(((bf16[4,24,16,512]{3,2,1,0:T(8,128)(2,1)}), bf16[4,24,16,512]{3,2,1,0:T(8,128)(2,1)S(1)}, u32[]{:S(2)}, u32[]{:S(2)}) %all-to-all-start.3) | async-done | bytes 1572896 | tf_op jit(solution)/shard_map/all_to_all | solution.py:47
  225.4 1.5 gather_fusion.3
  226.9 2.5 %convert_element_type.25 = f32[48,16,512]{2,1,0:T(8,128)} convert(bf16[48,16,512]{2,1,0:T(8,128)(2,1)} %gather_fusion.3) | non-fusion elementwise | flops 393216 | bytes 2359296 | tf_op jit(solution)/shard_map/convert_element_type | solution.py:49
  (21 shorter events, 1.1 us)
Async XLA Ops:
  0.0 9.6 %copy-start = (bf16[48,16,1024]{2,1,0:T(8,128)(2,1)S(1)}, bf16[48,16,1024]{2,1,0:T(8,128)(2,1)}, u32[]{:S(2)}) copy-start(bf16[48,16,1024]{2,1,0:T(8,128)(2,1)} %param.4) | copy-start | bytes 4718596
  2.5 11.7 %all-to-all-start.1 = ((s32[4,1,1]{2,1,0:T(1,128)}), s32[4,1,1]{2,1,0:T(1,128)S(1)}, u32[]{:S(2)}, u32[]{:S(2)}) async-start(s32[4,1,1]{2,1,0:T(1,128)} %copy.12), calls=%async_computation.1 | async-start | bytes 4096 | tf_op jit(solution)/shard_map/all_to_all | solution.py:27
  14.2 39.5 %all-to-all-start = ((bf16[4,24,16,512]{3,2,1,0:T(8,128)(2,1)}), bf16[4,24,16,512]{3,2,1,0:T(8,128)(2,1)S(1)}, u32[]{:S(2)}, u32[]{:S(2)}) async-start(bf16[4,24,16,512]{3,2,1,0:T(8,128)(2,1)} %bitcast.46), calls=%async_computation | async-start | bytes 3145728 | tf_op jit(solution)/shard_map/all_to_all | solution.py:25
  53.7 75.7 %all-to-all-start.2 = ((bf16[2,2,786432]{2,1,0:T(2,128)(2,1)}), bf16[2,2,786432]{2,1,0:T(2,128)(2,1)}, u32[]{:S(2)}, u32[]{:S(2)}) async-start(bf16[2,2,786432]{2,1,0:T(2,128)(2,1)} %reshape.176), calls=%async_computation.2 | async-start | bytes 12582912 | tf_op jit(solution)/shard_map/all_to_all | solution.py:14
  147.7 14.2 %copy-start.1 = (bf16[48,16,512]{2,1,0:T(8,128)(2,1)S(1)}, bf16[48,16,512]{2,1,0:T(8,128)(2,1)}, u32[]{:S(2)}) copy-start(bf16[48,16,512]{2,1,0:T(8,128)(2,1)} %gather_fusion.1) | copy-start | bytes 2359300
  190.6 34.8 %all-to-all-start.3 = ((bf16[4,24,16,512]{3,2,1,0:T(8,128)(2,1)}), bf16[4,24,16,512]{3,2,1,0:T(8,128)(2,1)S(1)}, u32[]{:S(2)}, u32[]{:S(2)}) async-start(bf16[4,24,16,512]{3,2,1,0:T(8,128)(2,1)} %bitcast.47), calls=%async_computation.3 | async-start | bytes 3145728 | tf_op jit(solution)/shard_map/all_to_all | solution.py:47

commit v2 on v1

v2 whole, which is shorter than its diff:
```python
import functools

import jax
import jax.numpy as jnp
from jax import lax
from jax.experimental import pallas as pl
from jax.experimental.pallas import tpu as pltpu
from jax.sharding import PartitionSpec as P

MESH = pl.DeviceIdType.MESH


def divisor(total, choices):
    for c in choices:
        if total % c == 0:
            return c
    return 1


def exchange(
    npairs,
    nsub,
    nrep,
    chunks,
    src_ref,
    out_ids_ref,
    counts_ref,
    integrals_ref,
    density_ref,
    out_ref,
    ints,
    den,
    pack,
    arrived,
    ret,
    homeward,
    counts_all,
    counts_smem,
    starts_smem,
    places_smem,
    fit_plane,
    fit_pairs,
    local_sem,
    own_sem,
    ints_send,
    ints_recv,
    den_send,
    den_recv,
    ret_send,
    ret_recv,
    cnt_send,
    cnt_recv,
    plane_send,
    plane_recv,
    pairs_send,
    pairs_recv,
):
    me = lax.axis_index("pairs")
    sub = lax.axis_index("sub")
    rep = lax.axis_index("rep")
    blocks, dens, _ = density_ref.shape
    xq = ints.shape[3]
    cap = arrived.shape[1] // npairs
    step = blocks // chunks

    def device(pair, s, r):
        return {"pairs": pair, "sub": s, "rep": r}

    def quarter(s, r):
        return pl.ds(pl.multiple_of((s * nrep + r) * xq, 128), xq)

    den_copy = pltpu.make_async_copy(
        density_ref.at[:, :, pl.ds(pl.multiple_of(sub * (nrep * xq), 128), nrep * xq)],
        den,
        local_sem,
    )
    den_copy.start()
    own_copy = pltpu.make_async_copy(
        integrals_ref.at[:, :, quarter(sub, rep)], ints.at[sub], own_sem
    )
    own_copy.start()

    pair_order = [lax.rem(me + npairs // 2 + i, npairs) for i in range(npairs - npairs // 2)] + [
        lax.rem(me + i, npairs) for i in range(1, npairs // 2)
    ]
    pair_peers = pair_order
    sub_peers = [lax.rem(sub + i, nsub) for i in range(1, nsub)]
    rep_peers = [lax.rem(rep + i, nrep) for i in range(1, nrep)]
    plane_peers = (
        [(sub, r) for r in rep_peers]
        + [(s, rep) for s in sub_peers]
        + [(s, r) for s in sub_peers for r in rep_peers]
    )

    barrier = pltpu.get_barrier_semaphore()
    greeted = 0
    for pair in pair_peers:
        for r in [rep] + rep_peers:
            pl.semaphore_signal(
                barrier, inc=1, device_id=device(pair, sub, r), device_id_type=MESH
            )
            greeted += 1
    for s, r in plane_peers:
        pl.semaphore_signal(barrier, inc=1, device_id=device(me, s, r), device_id_type=MESH)
        greeted += 1
    pl.semaphore_wait(barrier, greeted)

    def ints_copy(s, c, slot):
        return pltpu.make_async_remote_copy(
            src_ref=integrals_ref.at[pl.ds(c * step, step), :, quarter(s, rep)],
            dst_ref=ints.at[slot, pl.ds(c * step, step)],
            send_sem=ints_send.at[s, c],
            recv_sem=ints_recv.at[slot, c],
            device_id=device(me, s, rep),
            device_id_type=MESH,
        )

    for c in range(chunks):
        for s in sub_peers:
            ints_copy(s, c, sub).start()

    def cnt_copy(pair, slot):
        return pltpu.make_async_remote_copy(
            src_ref=counts_ref,
            dst_ref=counts_all.at[slot],
            send_sem=cnt_send.at[pair],
            recv_sem=cnt_recv.at[slot],
            device_id=device(pair, sub, rep),
            device_id_type=MESH,
        )

    for pair in pair_peers:
        cnt_copy(pair, me).start()
    counts_all[me] = counts_ref[...]

    den_copy.wait()

    def den_send_copy(pair, h, slot_pair, slot_rep):
        return pltpu.make_async_remote_copy(
            src_ref=pack.at[pair, h],
            dst_ref=arrived.at[slot_rep, pl.ds(slot_pair * cap, cap)],
            send_sem=den_send.at[pair, h],
            recv_sem=den_recv.at[slot_pair, slot_rep],
            device_id=device(pair, sub, h),
            device_id_type=MESH,
        )

    unroll = divisor(cap, (8, 6, 4, 3, 2))

    def pack_for(pair):
        def body(i, carry):
            for u in range(unroll):
                r = i * unroll + u
                k = src_ref[pair * cap + r]
                row = den[k]
                for h in range(nrep):
                    pack[pair, h, r] = row[:, h * xq : (h + 1) * xq]
            return carry

        lax.fori_loop(0, cap // unroll, body, 0)

    for pair in pair_order:
        pack_for(pair)
        for h in [rep] + rep_peers:
            den_send_copy(pair, h, me, rep).start()
    pack_for(me)
    for h in rep_peers:
        den_send_copy(me, h, me, rep).start()
    own_den = pltpu.make_async_copy(
        pack.at[me, rep], arrived.at[rep, pl.ds(me * cap, cap)], local_sem
    )
    own_den.start()

    for pair in pair_peers:
        cnt_copy(pair, pair).wait_recv()
    to_smem = pltpu.make_async_copy(counts_all, counts_smem, den_send.at[me, rep])
    to_smem.start()
    to_smem.wait()
    starts = []
    finish = []
    total = jnp.int32(0)
    for s in range(npairs):
        starts.append(total)
        starts_smem[s] = total
        total = total + counts_smem[s, 0, me]
        finish.append(total)

    def place(j, carry):
        anchor = jnp.int32(0)
        start = jnp.int32(0)
        for s in range(npairs - 1):
            past = j >= finish[s]
            anchor = anchor + jnp.where(past, 1, 0)
            start = jnp.where(past, finish[s], start)
        places_smem[j] = jnp.minimum(anchor * cap + j - start, npairs * cap - 1)
        return carry

    lax.fori_loop(0, blocks, place, 0)

    own_den.wait()
    own_copy.wait()
    for h in rep_peers:
        den_send_copy(me, rep, me, h).wait_recv()
    for pair in reversed(pair_order):
        for h in [rep] + rep_peers:
            den_send_copy(pair, rep, pair, h).wait_recv()

    def block_ints(j):
        return jnp.concatenate([ints[s, j] for s in range(nsub)], axis=0)

    fit_unroll = divisor(step, (12, 8, 6, 4, 3, 2))
    fit = jnp.zeros(fit_pairs.shape[1:], jnp.float32)
    for c in range(chunks):
        for s in sub_peers:
            ints_copy(s, c, s).wait_recv()

        def fit_body(i, acc):
            for u in range(fit_unroll):
                j = c * step + i * fit_unroll + u
                at = places_smem[j]
                rows = jnp.concatenate([arrived[h, at] for h in range(nrep)], axis=0)
                acc = acc + lax.dot_general(
                    rows,
                    block_ints(j),
                    (((1,), (1,)), ((), ())),
                    preferred_element_type=jnp.float32,
                )
            return acc

        fit = lax.fori_loop(0, step // fit_unroll, fit_body, fit)

    plane_me = sub * nrep + rep
    fit_plane[plane_me] = fit

    def plane_copy(s, r, slot):
        return pltpu.make_async_remote_copy(
            src_ref=fit_plane.at[plane_me],
            dst_ref=fit_plane.at[slot],
            send_sem=plane_send.at[s * nrep + r],
            recv_sem=plane_recv.at[slot],
            device_id=device(me, s, r),
            device_id_type=MESH,
        )

    for s, r in plane_peers:
        plane_copy(s, r, plane_me).start()
    for s, r in plane_peers:
        plane_copy(s, r, s * nrep + r).wait_recv()
    fit = fit_plane[0]
    for i in range(1, nsub * nrep):
        fit = fit + fit_plane[i]
    fit_pairs[me] = fit

    def pairs_copy(pair, slot):
        return pltpu.make_async_remote_copy(
            src_ref=fit_pairs.at[me],
            dst_ref=fit_pairs.at[slot],
            send_sem=pairs_send.at[pair],
            recv_sem=pairs_recv.at[slot],
            device_id=device(pair, sub, rep),
            device_id_type=MESH,
        )

    for pair in pair_peers:
        pairs_copy(pair, me).start()
    for pair in pair_peers:
        pairs_copy(pair, pair).wait_recv()
    fit = fit_pairs[0]
    for i in range(1, npairs):
        fit = fit + fit_pairs[i]
    fitted = fit.astype(jnp.bfloat16)

    def ret_copy(pair, h, slot_pair, slot_rep):
        return pltpu.make_async_remote_copy(
            src_ref=ret.at[pair, h],
            dst_ref=homeward.at[slot_rep, pl.ds(slot_pair * cap, cap)],
            send_sem=ret_send.at[pair, h],
            recv_sem=ret_recv.at[slot_pair, slot_rep],
            device_id=device(pair, sub, h),
            device_id_type=MESH,
        )

    def coulomb_for(pair):
        start = starts_smem[pair]

        def body(i, carry):
            for u in range(unroll):
                r = i * unroll + u
                j = jnp.minimum(start + r, blocks - 1)
                rows = jnp.dot(
                    fitted, block_ints(j), preferred_element_type=jnp.float32
                ).astype(jnp.bfloat16)
                for h in range(nrep):
                    ret[pair, h, r] = rows[h * dens : (h + 1) * dens]
            return carry

        lax.fori_loop(0, cap // unroll, body, 0)

    for pair in pair_order:
        coulomb_for(pair)
        for h in [rep] + rep_peers:
            ret_copy(pair, h, me, rep).start()
    coulomb_for(me)
    for h in rep_peers:
        ret_copy(me, h, me, rep).start()
    own_ret = pltpu.make_async_copy(
        ret.at[me, rep], homeward.at[rep, pl.ds(me * cap, cap)], local_sem
    )
    own_ret.start()

    for c in range(chunks):
        for s in sub_peers:
            ints_copy(s, c, sub).wait_send()
    for pair in pair_peers:
        cnt_copy(pair, me).wait_send()
        pairs_copy(pair, me).wait_send()
    for s, r in plane_peers:
        plane_copy(s, r, plane_me).wait_send()
    for pair in pair_peers:
        for h in [rep] + rep_peers:
            den_send_copy(pair, h, me, rep).wait_send()
    for h in rep_peers:
        den_send_copy(me, h, me, rep).wait_send()

    own_ret.wait()
    for h in rep_peers:
        ret_copy(me, rep, me, h).wait_recv()
    for pair in reversed(pair_order):
        for h in [rep] + rep_peers:
            ret_copy(pair, rep, pair, h).wait_recv()

    out_unroll = divisor(blocks, (8, 6, 4, 3, 2))

    def out_body(i, carry):
        for u in range(out_unroll):
            k = i * out_unroll + u
            at = out_ids_ref[k]
            out_ref[k] = jnp.concatenate([homeward[h, at] for h in range(nrep)], axis=1)
        return carry

    lax.fori_loop(0, blocks // out_unroll, out_body, 0)

    for pair in pair_peers:
        for h in [rep] + rep_peers:
            ret_copy(pair, h, me, rep).wait_send()
    for h in rep_peers:
        ret_copy(me, h, me, rep).wait_send()


def on_device(integrals, density, block_owner):
    npairs = lax.axis_size("pairs")
    nsub = lax.axis_size("sub")
    nrep = lax.axis_size("rep")
    blocks, dens, width = density.shape
    p_dev = integrals.shape[1]
    xq = width // (nsub * nrep)
    cap = 2 * blocks // npairs
    chunks = divisor(blocks, (4, 3, 2))
    peer_ids = jnp.arange(npairs, dtype=jnp.int32)
    onehot = (block_owner[:, None] == peer_ids[None, :]).astype(jnp.int32)
    before = jnp.cumsum(onehot, axis=0) - onehot
    rank_in = jnp.sum(before * onehot, axis=1)
    outgoing = block_owner * cap + rank_in
    buffer_ids = jnp.arange(npairs * cap, dtype=jnp.int32)
    matches = (outgoing[None, :] == buffer_ids[:, None]).astype(jnp.int32)
    source_ids = jnp.sum(matches * jnp.arange(blocks, dtype=jnp.int32)[None, :], axis=1)
    lanes = jnp.arange(128, dtype=jnp.int32)
    counts = jnp.sum((block_owner[:, None] == lanes[None, :]).astype(jnp.int32), axis=0)
    counts = jnp.broadcast_to(counts[None, :], (8, 128))

    vmem = pl.BlockSpec(memory_space=pltpu.VMEM)
    smem = pl.BlockSpec(memory_space=pltpu.SMEM)
    anywhere = pl.BlockSpec(memory_space=pl.ANY)
    bf16 = jnp.bfloat16
    sems = pltpu.SemaphoreType.DMA
    rows = pl.pallas_call(
        functools.partial(exchange, npairs, nsub, nrep, chunks),
        out_shape=jax.ShapeDtypeStruct((blocks, dens, nrep * xq), bf16),
        in_specs=[smem, smem, vmem, anywhere, anywhere],
        out_specs=vmem,
        scratch_shapes=[
            pltpu.VMEM((nsub, blocks, p_dev, xq), bf16),
            pltpu.VMEM((blocks, dens, nrep * xq), bf16),
            pltpu.VMEM((npairs, nrep, cap, dens, xq), bf16),
            pltpu.VMEM((nrep, npairs * cap, dens, xq), bf16),
            pltpu.VMEM((npairs, nrep, cap, dens, xq), bf16),
            pltpu.VMEM((nrep, npairs * cap, dens, xq), bf16),
            pltpu.VMEM((npairs, 8, 128), jnp.int32),
            pltpu.SMEM((npairs, 8, 128), jnp.int32),
            pltpu.SMEM((npairs,), jnp.int32),
            pltpu.SMEM((blocks,), jnp.int32),
            pltpu.VMEM((nsub * nrep, nrep * dens, nsub * p_dev), jnp.float32),
            pltpu.VMEM((npairs, nrep * dens, nsub * p_dev), jnp.float32),
            sems,
            sems,
            sems((nsub, chunks)),
            sems((nsub, chunks)),
            sems((npairs, nrep)),
            sems((npairs, nrep)),
            sems((npairs, nrep)),
            sems((npairs, nrep)),
            sems((npairs,)),
            sems((npairs,)),
            sems((nsub * nrep,)),
            sems((nsub * nrep,)),
            sems((npairs,)),
            sems((npairs,)),
        ],
        compiler_params=pltpu.CompilerParams(
            collective_id=0, has_side_effects=True, vmem_limit_bytes=40 * 1024 * 1024
        ),
    )(source_ids, outgoing, counts, integrals, density)
    return rows.astype(jnp.float32)


def solution(mesh):
    in_specs = (
        P(("groups", "pairs"), "sub", None),
        P(("groups", "pairs"), "rep", None),
        P(("groups", "pairs")),
    )
    out_specs = P(("groups", "pairs"), "rep", "sub")
    return jax.shard_map(
        on_device, mesh=mesh, in_specs=in_specs, out_specs=out_specs, check_vma=False
    )
```

time: 231 us -> 92.3 us (0.40)
  the two profiles are of different devices: /device:TPU:0 before, /device:TPU:9 now
where the time goes in v2:
time: 92.3 us; the launch traced here: 92.1 us
  Pallas kernels  83.4 us (90%)
  other arithmetic  4.5 us (5%)
  local copies, waits for them, and re-layouts  4.2 us (5%)
    pallas_call x1, Pallas kernels, on_device(): pl.pallas_call(functools.partial(exchange, npairs, nsub, nrep, chunks), o...  83.4 us
    unnamed x4, local copies, waits for them, and re-layouts  4.19 us

profile of v2, /device:TPU:9, one launch (start us, length us, event | category | flops | bytes accessed | tf_op | source)
XLA Modules:
  0.0 92.1 jit_solution(7275441158403731637)
XLA Ops:
  0.0 0.7 convert_reduce_fusion
  0.8 0.7 fusion
  1.5 0.1 reduce_window_sum.11
  1.6 0.8 select_reduce_fusion.1
  2.4 0.7 multiply_add_fusion.out_ids_ref
  3.1 0.1 select_reduce_fusion.src_ref
  3.2 0.0 copy-start
  3.2 2.8 %copy-done = bf16[48,64,1024]{2,1,0:T(8,128)(2,1)S(1)} copy-done((bf16[48,64,1024]{2,1,0:T(8,128)(2,1)S(1)}, bf16[48,64,1024]{2,1,0:T(8,128)(2,1)}, u32[]{:S(2)}) %copy-start) | copy-done | bytes 6291480
  5.9 0.0 copy-start.1
  5.9 1.4 %copy-done.1 = bf16[48,16,1024]{2,1,0:T(8,128)(2,1)S(1)} copy-done((bf16[48,16,1024]{2,1,0:T(8,128)(2,1)S(1)}, bf16[48,16,1024]{2,1,0:T(8,128)(2,1)}, u32[]{:S(2)}) %copy-start.1) | copy-done | bytes 1572888
  7.3 83.4 %shard_map.37 = bf16[48,16,512]{2,1,0:T(8,128)(2,1)S(1)} custom-call(s32[96]{0:T(128)S(1)} %select_reduce_fusion.src_ref, s32[48]{0:T(128)S(1)} %multiply_add_fusion.out_ids_ref, s32[8,128]{1,0:T(8,128)S(1)} %broadcast_in_dim.2.counts_ref, bf16[48,64,1024]{2,1,0:T(8,128)(2,1)S(1)} %copy-done, bf16[48,16,1024]{2,1,0:T(8,128)(2,1)S(1)} %copy-done.1), custom_call_target="tpu_custom_call" | custom-call | tf_op jit(solution)/shard_map/pallas_call | solution.py:376
  90.7 1.4 %convert_element_type.12 = f32[48,16,512]{2,1,0:T(8,128)} convert(bf16[48,16,512]{2,1,0:T(8,128)(2,1)S(1)} %shard_map.37) | non-fusion elementwise | flops 393216 | bytes 2359296 | tf_op jit(solution)/shard_map/convert_element_type | solution.py:413
  (1 shorter events, 0.0 us)
Async XLA Ops:
  3.2 2.8 %copy-start = (bf16[48,64,1024]{2,1,0:T(8,128)(2,1)S(1)}, bf16[48,64,1024]{2,1,0:T(8,128)(2,1)}, u32[]{:S(2)}) copy-start(bf16[48,64,1024]{2,1,0:T(8,128)(2,1)} %integrals_ref.1) | copy-start | bytes 18874372
  5.9 1.4 %copy-start.1 = (bf16[48,16,1024]{2,1,0:T(8,128)(2,1)S(1)}, bf16[48,16,1024]{2,1,0:T(8,128)(2,1)}, u32[]{:S(2)}) copy-start(bf16[48,16,1024]{2,1,0:T(8,128)(2,1)} %density_ref.1) | copy-start | bytes 4718596

commit v3 on v2

--- a/solution.py
+++ b/solution.py
@@ -22,9 +22,7 @@
     nsub,
     nrep,
     chunks,
-    src_ref,
-    out_ids_ref,
-    counts_ref,
+    owner_ref,
     integrals_ref,
     density_ref,
     out_ref,
@@ -34,6 +32,8 @@
     arrived,
     ret,
     homeward,
+    out_ids_ref,
+    next_smem,
     counts_all,
     counts_smem,
     starts_smem,
@@ -103,6 +103,59 @@
     for s, r in plane_peers:
         pl.semaphore_signal(barrier, inc=1, device_id=device(me, s, r), device_id_type=MESH)
         greeted += 1
+
+    peer_range = range(npairs)
+
+    def rank_body(k, seen):
+        owner = owner_ref[k]
+        at = owner * cap
+        after = []
+        for o in peer_range:
+            mine = owner == o
+            at = at + jnp.where(mine, seen[o], 0)
+            after.append(seen[o] + jnp.where(mine, 1, 0))
+        out_ids_ref[k] = at
+        return tuple(after)
+
+    sent = lax.fori_loop(0, blocks, rank_body, (jnp.int32(0),) * npairs)
+
+    for o in peer_range:
+        next_smem[o, blocks] = jnp.int32(blocks)
+
+    def next_body(i, following):
+        k = blocks - 1 - i
+        owner = owner_ref[k]
+        found = []
+        for o in peer_range:
+            found.append(jnp.where(owner == o, k, following[o]))
+            next_smem[o, k] = found[o]
+        return tuple(found)
+
+    lax.fori_loop(0, blocks, next_body, (jnp.int32(blocks),) * npairs)
+
+    lanes = lax.broadcasted_iota(jnp.int32, counts_all.shape[1:], 1)
+    sent_row = jnp.zeros(counts_all.shape[1:], jnp.int32)
+    for o in peer_range:
+        sent_row = jnp.where(lanes == o, sent[o], sent_row)
+    counts_all[me] = sent_row
+
+    unroll = divisor(cap, (8, 6, 4, 3, 2))
+
+    def pack_for(pair):
+        def body(i, k):
+            for u in range(unroll):
+                r = i * unroll + u
+                row = den[jnp.minimum(k, blocks - 1)]
+                for h in range(nrep):
+                    pack[pair, h, r] = row[:, h * xq : (h + 1) * xq]
+                k = next_smem[pair, jnp.minimum(k + 1, blocks)]
+            return k
+
+        lax.fori_loop(0, cap // unroll, body, next_smem[pair, 0])
+
+    den_copy.wait()
+    for pair in pair_order:
+        pack_for(pair)
     pl.semaphore_wait(barrier, greeted)
 
     def ints_copy(s, c, slot):
@@ -115,25 +168,15 @@
             device_id_type=MESH,
         )
 
-    for c in range(chunks):
-        for s in sub_peers:
-            ints_copy(s, c, sub).start()
-
     def cnt_copy(pair, slot):
         return pltpu.make_async_remote_copy(
-            src_ref=counts_ref,
+            src_ref=counts_all.at[me],
             dst_ref=counts_all.at[slot],
             send_sem=cnt_send.at[pair],
             recv_sem=cnt_recv.at[slot],
             device_id=device(pair, sub, rep),
             device_id_type=MESH,
         )
-
-    for pair in pair_peers:
-        cnt_copy(pair, me).start()
-    counts_all[me] = counts_ref[...]
-
-    den_copy.wait()
 
     def den_send_copy(pair, h, slot_pair, slot_rep):
         return pltpu.make_async_remote_copy(
@@ -145,24 +188,14 @@
             device_id_type=MESH,
         )
 
-    unroll = divisor(cap, (8, 6, 4, 3, 2))
-
-    def pack_for(pair):
-        def body(i, carry):
-            for u in range(unroll):
-                r = i * unroll + u
-                k = src_ref[pair * cap + r]
-                row = den[k]
-                for h in range(nrep):
-                    pack[pair, h, r] = row[:, h * xq : (h + 1) * xq]
-            return carry
-
-        lax.fori_loop(0, cap // unroll, body, 0)
-
+    for pair in pair_peers:
+        cnt_copy(pair, me).start()
     for pair in pair_order:
-        pack_for(pair)
         for h in [rep] + rep_peers:
             den_send_copy(pair, h, me, rep).start()
+    for c in range(chunks):
+        for s in sub_peers:
+            ints_copy(s, c, sub).start()
     pack_for(me)
     for h in rep_peers:
         den_send_copy(me, h, me, rep).start()
@@ -356,27 +389,15 @@
     xq = width // (nsub * nrep)
     cap = 2 * blocks // npairs
     chunks = divisor(blocks, (4, 3, 2))
-    peer_ids = jnp.arange(npairs, dtype=jnp.int32)
-    onehot = (block_owner[:, None] == peer_ids[None, :]).astype(jnp.int32)
-    before = jnp.cumsum(onehot, axis=0) - onehot
-    rank_in = jnp.sum(before * onehot, axis=1)
-    outgoing = block_owner * cap + rank_in
-    buffer_ids = jnp.arange(npairs * cap, dtype=jnp.int32)
-    matches = (outgoing[None, :] == buffer_ids[:, None]).astype(jnp.int32)
-    source_ids = jnp.sum(matches * jnp.arange(blocks, dtype=jnp.int32)[None, :], axis=1)
-    lanes = jnp.arange(128, dtype=jnp.int32)
-    counts = jnp.sum((block_owner[:, None] == lanes[None, :]).astype(jnp.int32), axis=0)
-    counts = jnp.broadcast_to(counts[None, :], (8, 128))
-
     vmem = pl.BlockSpec(memory_space=pltpu.VMEM)
     smem = pl.BlockSpec(memory_space=pltpu.SMEM)
-    anywhere = pl.BlockSpec(memory_space=pl.ANY)
+    hbm = pl.BlockSpec(memory_space=pltpu.HBM)
     bf16 = jnp.bfloat16
     sems = pltpu.SemaphoreType.DMA
     rows = pl.pallas_call(
         functools.partial(exchange, npairs, nsub, nrep, chunks),
         out_shape=jax.ShapeDtypeStruct((blocks, dens, nrep * xq), bf16),
-        in_specs=[smem, smem, vmem, anywhere, anywhere],
+        in_specs=[smem, hbm, hbm],
         out_specs=vmem,
         scratch_shapes=[
             pltpu.VMEM((nsub, blocks, p_dev, xq), bf16),
@@ -385,6 +406,8 @@
             pltpu.VMEM((nrep, npairs * cap, dens, xq), bf16),
             pltpu.VMEM((npairs, nrep, cap, dens, xq), bf16),
             pltpu.VMEM((nrep, npairs * cap, dens, xq), bf16),
+            pltpu.SMEM((blocks,), jnp.int32),
+            pltpu.SMEM((npairs, blocks + 1), jnp.int32),
             pltpu.VMEM((npairs, 8, 128), jnp.int32),
             pltpu.SMEM((npairs, 8, 128), jnp.int32),
             pltpu.SMEM((npairs,), jnp.int32),
@@ -407,9 +430,9 @@
             sems((npairs,)),
         ],
         compiler_params=pltpu.CompilerParams(
-            collective_id=0, has_side_effects=True, vmem_limit_bytes=40 * 1024 * 1024
+            collective_id=0, has_side_effects=True, vmem_limit_bytes=56 * 1024 * 1024
         ),
-    )(source_ids, outgoing, counts, integrals, density)
+    )(block_owner, integrals, density)
     return rows.astype(jnp.float32)
 
 

time: 92.3 us -> 86.8 us (0.940)
  local copies, waits for them, and re-layouts: 4.2 us -> 0 us
  other arithmetic: 4.5 us -> 2.49 us
    unnamed x4 -> x0, local copies, waits for them, and re-layouts: 4.19 us -> none
    reduce_sum x3 -> x0, other arithmetic: 1.67 us -> none  [the longest x1 0.83 us: on_device(): rank_in = jnp.sum(before * onehot, axis=1)]
    convert_element_type x1, other arithmetic: 1.35 us -> 2.49 us  [on_device(): return rows.astype(jnp.float32)]
where the time goes in v3:
time: 86.8 us; the launch traced here: 86.7 us
  Pallas kernels  84.2 us (97%)
  other arithmetic  2.49 us (3%)
    pallas_call x1, Pallas kernels, on_device(): pl.pallas_call(functools.partial(exchange, npairs, nsub, nrep, chunks), o...  84.2 us
    convert_element_type x1, other arithmetic, on_device(): return rows.astype(jnp.float32)  2.49 us

profile of v3, /device:TPU:9, one launch (start us, length us, event | category | flops | bytes accessed | tf_op | source)
XLA Modules:
  0.0 86.7 jit_solution(18211402773323210062)
XLA Ops:
  0.0 84.2 %shard_map.37 = bf16[48,16,512]{2,1,0:T(8,128)(2,1)} custom-call(s32[48]{0:T(128)} %owner_ref.1, bf16[48,64,1024]{2,1,0:T(8,128)(2,1)} %integrals_ref.1, bf16[48,16,1024]{2,1,0:T(8,128)(2,1)} %density_ref.1), custom_call_target="tpu_custom_call" | custom-call | tf_op jit(solution)/shard_map/pallas_call | solution.py:397
  84.2 2.5 %convert_element_type.3 = f32[48,16,512]{2,1,0:T(8,128)} convert(bf16[48,16,512]{2,1,0:T(8,128)(2,1)} %shard_map.37) | non-fusion elementwise | flops 393216 | bytes 2359296 | tf_op jit(solution)/shard_map/convert_element_type | solution.py:436

commit v4 on v3

--- a/solution.py
+++ b/solution.py
@@ -154,8 +154,7 @@
         lax.fori_loop(0, cap // unroll, body, next_smem[pair, 0])
 
     den_copy.wait()
-    for pair in pair_order:
-        pack_for(pair)
+    pack_for(pair_order[0])
     pl.semaphore_wait(barrier, greeted)
 
     def ints_copy(s, c, slot):
@@ -190,12 +189,15 @@
 
     for pair in pair_peers:
         cnt_copy(pair, me).start()
-    for pair in pair_order:
+    for i, pair in enumerate(pair_order):
+        if i > 0:
+            pack_for(pair)
         for h in [rep] + rep_peers:
             den_send_copy(pair, h, me, rep).start()
-    for c in range(chunks):
-        for s in sub_peers:
-            ints_copy(s, c, sub).start()
+        if i == 0:
+            for c in range(chunks):
+                for s in sub_peers:
+                    ints_copy(s, c, sub).start()
     pack_for(me)
     for h in rep_peers:
         den_send_copy(me, h, me, rep).start()

time: 86.8 us -> 86.8 us (level)
  no operation moved by 1% of the time
where the time goes in v4:
time: 86.8 us; the launch traced here: 86.7 us
  Pallas kernels  84.2 us (97%)
  other arithmetic  2.49 us (3%)
    pallas_call x1, Pallas kernels, on_device(): pl.pallas_call(functools.partial(exchange, npairs, nsub, nrep, chunks), o...  84.2 us
    convert_element_type x1, other arithmetic, on_device(): return rows.astype(jnp.float32)  2.49 us

profile of v4, /device:TPU:9, one launch (start us, length us, event | category | flops | bytes accessed | tf_op | source)
XLA Modules:
  0.0 86.7 jit_solution(9177850222854371898)
XLA Ops:
  0.0 84.2 %shard_map.37 = bf16[48,16,512]{2,1,0:T(8,128)(2,1)} custom-call(s32[48]{0:T(128)} %owner_ref.1, bf16[48,64,1024]{2,1,0:T(8,128)(2,1)} %integrals_ref.1, bf16[48,16,1024]{2,1,0:T(8,128)(2,1)} %density_ref.1), custom_call_target="tpu_custom_call" | custom-call | tf_op jit(solution)/shard_map/pallas_call | solution.py:399
  84.2 2.5 %convert_element_type.3 = f32[48,16,512]{2,1,0:T(8,128)} convert(bf16[48,16,512]{2,1,0:T(8,128)(2,1)} %shard_map.37) | non-fusion elementwise | flops 393216 | bytes 2359296 | tf_op jit(solution)/shard_map/convert_element_type | solution.py:438

commit v5 on v4

--- a/solution.py
+++ b/solution.py
@@ -432,7 +432,7 @@
             sems((npairs,)),
         ],
         compiler_params=pltpu.CompilerParams(
-            collective_id=0, has_side_effects=True, vmem_limit_bytes=56 * 1024 * 1024
+            collective_id=0, has_side_effects=True, vmem_limit_bytes=105 * 512 * 1024
         ),
     )(block_owner, integrals, density)
     return rows.astype(jnp.float32)

time: 86.8 us -> 85.3 us (0.983)
  other arithmetic: 2.49 us -> 1.35 us
  Pallas kernels: 84.2 us -> 83.2 us
    convert_element_type x1, other arithmetic: 2.49 us -> 1.35 us  [on_device(): return rows.astype(jnp.float32)]
    pallas_call x1, Pallas kernels: 84.2 us -> 83.2 us  [on_device(): pl.pallas_call(functools.partial(exchange, npairs, nsub, nrep, chunks), o...]
where the time goes in v5:
time: 85.3 us; the launch traced here: 85.2 us
  Pallas kernels  83.2 us (98%)
  other arithmetic  1.35 us (2%)
    pallas_call x1, Pallas kernels, on_device(): pl.pallas_call(functools.partial(exchange, npairs, nsub, nrep, chunks), o...  83.2 us

profile of v5, /device:TPU:9, one launch (start us, length us, event | category | flops | bytes accessed | tf_op | source)
XLA Modules:
  0.0 85.2 jit_solution(5552423266115891025)
XLA Ops:
  0.0 0.0 copy-start
  0.0 0.7 copy-done
  0.7 83.2 %shard_map.37 = bf16[48,16,512]{2,1,0:T(8,128)(2,1)S(1)} custom-call(s32[48]{0:T(128)S(1)} %copy-done, bf16[48,64,1024]{2,1,0:T(8,128)(2,1)} %integrals_ref.1, bf16[48,16,1024]{2,1,0:T(8,128)(2,1)} %density_ref.1), custom_call_target="tpu_custom_call" | custom-call | tf_op jit(solution)/shard_map/pallas_call | solution.py:399
  83.8 1.4 %convert_element_type.3 = f32[48,16,512]{2,1,0:T(8,128)} convert(bf16[48,16,512]{2,1,0:T(8,128)(2,1)S(1)} %shard_map.37) | non-fusion elementwise | flops 393216 | bytes 2359296 | tf_op jit(solution)/shard_map/convert_element_type | solution.py:438
Async XLA Ops:
  0.0 0.7 copy-start

commit v6 on v5

--- a/solution.py
+++ b/solution.py
@@ -277,7 +277,7 @@
             device_id_type=MESH,
         )
 
-    for s, r in plane_peers:
+    for s, r in reversed(plane_peers):
         plane_copy(s, r, plane_me).start()
     for s, r in plane_peers:
         plane_copy(s, r, s * nrep + r).wait_recv()
@@ -305,22 +305,26 @@
         fit = fit + fit_pairs[i]
     fitted = fit.astype(jnp.bfloat16)
 
-    def ret_copy(pair, h, slot_pair, slot_rep):
-        return pltpu.make_async_remote_copy(
-            src_ref=ret.at[pair, h],
-            dst_ref=homeward.at[slot_rep, pl.ds(slot_pair * cap, cap)],
-            send_sem=ret_send.at[pair, h],
-            recv_sem=ret_recv.at[slot_pair, slot_rep],
+    pieces = ret_send.shape[2]
+    piece = cap // pieces
+    piece_unroll = divisor(piece, (6, 4, 3, 2))
+
+    def ret_copy(pair, h, part, slot_pair, slot_rep):
+        return pltpu.make_async_remote_copy(
+            src_ref=ret.at[pair, h, pl.ds(part * piece, piece)],
+            dst_ref=homeward.at[slot_rep, pl.ds(slot_pair * cap + part * piece, piece)],
+            send_sem=ret_send.at[pair, h, part],
+            recv_sem=ret_recv.at[slot_pair, slot_rep, part],
             device_id=device(pair, sub, h),
             device_id_type=MESH,
         )
 
-    def coulomb_for(pair):
+    def coulomb_for(pair, part):
         start = starts_smem[pair]
 
         def body(i, carry):
-            for u in range(unroll):
-                r = i * unroll + u
+            for u in range(piece_unroll):
+                r = part * piece + i * piece_unroll + u
                 j = jnp.minimum(start + r, blocks - 1)
                 rows = jnp.dot(
                     fitted, block_ints(j), preferred_element_type=jnp.float32
@@ -329,15 +333,17 @@
                     ret[pair, h, r] = rows[h * dens : (h + 1) * dens]
             return carry
 
-        lax.fori_loop(0, cap // unroll, body, 0)
+        lax.fori_loop(0, piece // piece_unroll, body, 0)
 
     for pair in pair_order:
-        coulomb_for(pair)
-        for h in [rep] + rep_peers:
-            ret_copy(pair, h, me, rep).start()
-    coulomb_for(me)
-    for h in rep_peers:
-        ret_copy(me, h, me, rep).start()
+        for part in range(pieces):
+            coulomb_for(pair, part)
+            for h in [rep] + rep_peers:
+                ret_copy(pair, h, part, me, rep).start()
+    for part in range(pieces):
+        coulomb_for(me, part)
+        for h in rep_peers:
+            ret_copy(me, h, part, me, rep).start()
     own_ret = pltpu.make_async_copy(
         ret.at[me, rep], homeward.at[rep, pl.ds(me * cap, cap)], local_sem
     )
@@ -358,11 +364,13 @@
         den_send_copy(me, h, me, rep).wait_send()
 
     own_ret.wait()
-    for h in rep_peers:
-        ret_copy(me, rep, me, h).wait_recv()
+    for part in range(pieces):
+        for h in rep_peers:
+            ret_copy(me, rep, part, me, h).wait_recv()
     for pair in reversed(pair_order):
-        for h in [rep] + rep_peers:
-            ret_copy(pair, rep, pair, h).wait_recv()
+        for part in range(pieces):
+            for h in [rep] + rep_peers:
+                ret_copy(pair, rep, part, pair, h).wait_recv()
 
     out_unroll = divisor(blocks, (8, 6, 4, 3, 2))
 
@@ -375,11 +383,12 @@
 
     lax.fori_loop(0, blocks // out_unroll, out_body, 0)
 
-    for pair in pair_peers:
-        for h in [rep] + rep_peers:
-            ret_copy(pair, h, me, rep).wait_send()
-    for h in rep_peers:
-        ret_copy(me, h, me, rep).wait_send()
+    for part in range(pieces):
+        for pair in pair_peers:
+            for h in [rep] + rep_peers:
+                ret_copy(pair, h, part, me, rep).wait_send()
+        for h in rep_peers:
+            ret_copy(me, h, part, me, rep).wait_send()
 
 
 def on_device(integrals, density, block_owner):
@@ -391,6 +400,7 @@
     xq = width // (nsub * nrep)
     cap = 2 * blocks // npairs
     chunks = divisor(blocks, (4, 3, 2))
+    pieces = divisor(cap, (2,))
     vmem = pl.BlockSpec(memory_space=pltpu.VMEM)
     smem = pl.BlockSpec(memory_space=pltpu.SMEM)
     hbm = pl.BlockSpec(memory_space=pltpu.HBM)
@@ -422,8 +432,8 @@
             sems((nsub, chunks)),
             sems((npairs, nrep)),
             sems((npairs, nrep)),
-            sems((npairs, nrep)),
-            sems((npairs, nrep)),
+            sems((npairs, nrep, pieces)),
+            sems((npairs, nrep, pieces)),
             sems((npairs,)),
             sems((npairs,)),
             sems((nsub * nrep,)),

time: 85.3 us -> 84.6 us (level)
  no operation moved by 1% of the time
where the time goes in v6:
time: 84.6 us; the launch traced here: 84.5 us
  Pallas kernels  82.5 us (98%)
  other arithmetic  1.35 us (2%)
    pallas_call x1, Pallas kernels, on_device(): pl.pallas_call(functools.partial(exchange, npairs, nsub, nrep, chunks), o...  82.5 us

profile of v6, /device:TPU:9, one launch (start us, length us, event | category | flops | bytes accessed | tf_op | source)
XLA Modules:
  0.0 84.5 jit_solution(9280753257851330117)
XLA Ops:
  0.0 0.0 copy-start
  0.0 0.7 copy-done
  0.7 82.5 %shard_map.37 = bf16[48,16,512]{2,1,0:T(8,128)(2,1)S(1)} custom-call(s32[48]{0:T(128)S(1)} %copy-done, bf16[48,64,1024]{2,1,0:T(8,128)(2,1)} %integrals_ref.1, bf16[48,16,1024]{2,1,0:T(8,128)(2,1)} %density_ref.1), custom_call_target="tpu_custom_call" | custom-call | tf_op jit(solution)/shard_map/pallas_call | solution.py:409
  83.1 1.4 %convert_element_type.3 = f32[48,16,512]{2,1,0:T(8,128)} convert(bf16[48,16,512]{2,1,0:T(8,128)(2,1)S(1)} %shard_map.37) | non-fusion elementwise | flops 393216 | bytes 2359296 | tf_op jit(solution)/shard_map/convert_element_type | solution.py:448
Async XLA Ops:
  0.0 0.7 copy-start

commit v7 on v6

--- a/solution.py
+++ b/solution.py
@@ -153,8 +153,6 @@
 
         lax.fori_loop(0, cap // unroll, body, next_smem[pair, 0])
 
-    den_copy.wait()
-    pack_for(pair_order[0])
     pl.semaphore_wait(barrier, greeted)
 
     def ints_copy(s, c, slot):
@@ -189,15 +187,14 @@
 
     for pair in pair_peers:
         cnt_copy(pair, me).start()
-    for i, pair in enumerate(pair_order):
-        if i > 0:
-            pack_for(pair)
+    for c in range(chunks):
+        for s in sub_peers:
+            ints_copy(s, c, sub).start()
+    den_copy.wait()
+    for pair in pair_order:
+        pack_for(pair)
         for h in [rep] + rep_peers:
             den_send_copy(pair, h, me, rep).start()
-        if i == 0:
-            for c in range(chunks):
-                for s in sub_peers:
-                    ints_copy(s, c, sub).start()
     pack_for(me)
     for h in rep_peers:
         den_send_copy(me, h, me, rep).start()

time: 84.6 us -> 84.6 us (level)
  no operation moved by 1% of the time
where the time goes in v7:
time: 84.6 us; the launch traced here: 84.5 us
  Pallas kernels  82.5 us (98%)
  other arithmetic  1.35 us (2%)
    pallas_call x1, Pallas kernels, on_device(): pl.pallas_call(functools.partial(exchange, npairs, nsub, nrep, chunks), o...  82.5 us

profile of v7, /device:TPU:9, one launch (start us, length us, event | category | flops | bytes accessed | tf_op | source)
XLA Modules:
  0.0 84.5 jit_solution(4952072900322912454)
XLA Ops:
  0.0 0.0 copy-start
  0.0 0.7 copy-done
  0.7 82.5 %shard_map.37 = bf16[48,16,512]{2,1,0:T(8,128)(2,1)S(1)} custom-call(s32[48]{0:T(128)S(1)} %copy-done, bf16[48,64,1024]{2,1,0:T(8,128)(2,1)} %integrals_ref.1, bf16[48,16,1024]{2,1,0:T(8,128)(2,1)} %density_ref.1), custom_call_target="tpu_custom_call" | custom-call | tf_op jit(solution)/shard_map/pallas_call | solution.py:406
  83.1 1.4 %convert_element_type.3 = f32[48,16,512]{2,1,0:T(8,128)} convert(bf16[48,16,512]{2,1,0:T(8,128)(2,1)S(1)} %shard_map.37) | non-fusion elementwise | flops 393216 | bytes 2359296 | tf_op jit(solution)/shard_map/convert_element_type | solution.py:445
Async XLA Ops:
  0.0 0.7 copy-start

commit v8 on v7

--- a/solution.py
+++ b/solution.py
@@ -261,6 +261,26 @@
 
         fit = lax.fori_loop(0, step // fit_unroll, fit_body, fit)
 
+    fit_pairs[me] = fit
+
+    def pairs_copy(pair, slot):
+        return pltpu.make_async_remote_copy(
+            src_ref=fit_pairs.at[me],
+            dst_ref=fit_pairs.at[slot],
+            send_sem=pairs_send.at[pair],
+            recv_sem=pairs_recv.at[slot],
+            device_id=device(pair, sub, rep),
+            device_id_type=MESH,
+        )
+
+    for pair in pair_peers:
+        pairs_copy(pair, me).start()
+    for pair in pair_peers:
+        pairs_copy(pair, pair).wait_recv()
+    fit = fit_pairs[0]
+    for i in range(1, npairs):
+        fit = fit + fit_pairs[i]
+
     plane_me = sub * nrep + rep
     fit_plane[plane_me] = fit
 
@@ -281,25 +301,6 @@
     fit = fit_plane[0]
     for i in range(1, nsub * nrep):
         fit = fit + fit_plane[i]
-    fit_pairs[me] = fit
-
-    def pairs_copy(pair, slot):
-        return pltpu.make_async_remote_copy(
-            src_ref=fit_pairs.at[me],
-            dst_ref=fit_pairs.at[slot],
-            send_sem=pairs_send.at[pair],
-            recv_sem=pairs_recv.at[slot],
-            device_id=device(pair, sub, rep),
-            device_id_type=MESH,
-        )
-
-    for pair in pair_peers:
-        pairs_copy(pair, me).start()
-    for pair in pair_peers:
-        pairs_copy(pair, pair).wait_recv()
-    fit = fit_pairs[0]
-    for i in range(1, npairs):
-        fit = fit + fit_pairs[i]
     fitted = fit.astype(jnp.bfloat16)
 
     pieces = ret_send.shape[2]

time: 84.6 us -> 85.6 us (1.012)
  Pallas kernels: 82.5 us -> 83.4 us
    pallas_call x1, Pallas kernels: 82.5 us -> 83.4 us  [on_device(): pl.pallas_call(functools.partial(exchange, npairs, nsub, nrep, chunks), o...]
where the time goes in v8:
time: 85.6 us; the launch traced here: 85.4 us
  Pallas kernels  83.4 us (97%)
  other arithmetic  1.35 us (2%)
    pallas_call x1, Pallas kernels, on_device(): pl.pallas_call(functools.partial(exchange, npairs, nsub, nrep, chunks), o...  83.4 us

profile of v8, /device:TPU:9, one launch (start us, length us, event | category | flops | bytes accessed | tf_op | source)
XLA Modules:
  0.0 85.4 jit_solution(15498715065580575721)
XLA Ops:
  0.0 0.0 copy-start
  0.0 0.7 copy-done
  0.7 83.4 %shard_map.37 = bf16[48,16,512]{2,1,0:T(8,128)(2,1)S(1)} custom-call(s32[48]{0:T(128)S(1)} %copy-done, bf16[48,64,1024]{2,1,0:T(8,128)(2,1)} %integrals_ref.1, bf16[48,16,1024]{2,1,0:T(8,128)(2,1)} %density_ref.1), custom_call_target="tpu_custom_call" | custom-call | tf_op jit(solution)/shard_map/pallas_call | solution.py:407
  84.1 1.4 %convert_element_type.3 = f32[48,16,512]{2,1,0:T(8,128)} convert(bf16[48,16,512]{2,1,0:T(8,128)(2,1)S(1)} %shard_map.37) | non-fusion elementwise | flops 393216 | bytes 2359296 | tf_op jit(solution)/shard_map/convert_element_type | solution.py:446
Async XLA Ops:
  0.0 0.7 copy-start
